TPU v7x, 32 devices: a whole 2x2x4 slice. The times are simulated.
32 devices in a mesh: groups: 2 (over y), wide: 4 (over z), narrow: 4 (over x, core).
Axes of the slice: x: 2, y: 2, z: 4, core: 2. Of those that a mesh axis runs over, the one named last changes fastest.
Arguments:
- cand_acts: bfloat16 [2048, 28672], P(('groups', 'narrow'), 'wide'), parts along dimension 0, may hold values from -6 to 6
- cand_grads: bfloat16 [2048, 8192], P(('groups', 'narrow'), 'wide'), parts along dimension 0, may hold values from -6 to 6
- query_acts: bfloat16 [512, 28672], P('groups', 'wide'), parts along dimension 0, may hold values from -6 to 6
- query_grads: bfloat16 [512, 8192], P('groups', 'wide'), parts along dimension 0, may hold values from -6 to 6
- basis_in: bfloat16 [28672, 512], P('wide'), may hold values from -0.03125 to 0.03125
- basis_out: bfloat16 [8192, 256], P('wide'), may hold values from -0.0625 to 0.0625
- eigvals: float32 [256, 512], P(None, 'wide'), may hold values from 0.25 to 4
- slot_pair: int32 [2048], P(('groups', 'narrow')), parts along dimension 0, may hold values from 0 to 128, as said below
Outputs:
- scores: float32 [256, 64], P(('groups', 'wide', 'narrow')), parts along dimension 0
There are 2 independent parts, one for each index of `groups`. A program takes and returns all parts, laid end to end along the dimension named above; an argument that names none is the same for every part. Nothing has to cross between parts.
Inputs may be any that keep to these rules, and one draw needn't show every extreme that they name: `slot_pair`: on each index of narrow the live slots (value below 128) come first among its 256 slots and the others hold 128. Live slots over all devices number exactly 512; read in device order their values never fall and every pair has one or more. In every draw the slots of some index of narrow are all live.
All inputs are finite; a program needn't handle non-finite values.
Results may differ from a plain program's by a relative error of at most 0.004.
Values may be sent and summed in bfloat16 or wider, within the bound.
A program may use at most 64 MiB of HBM per device.

v0:
```python
import math

import jax
import jax.numpy as jnp
from jax import lax
from jax.sharding import PartitionSpec as P

KG = 256
QUERIES = 64
QPER = 4
TOK_DEV = 128
PAIRS = 128


def per_device(
    cand_acts, cand_grads, query_acts, query_grads, basis_in, basis_out, eigvals, slot_pair
):
    narrow_count = lax.axis_size("narrow")
    wide_count = lax.axis_size("wide")
    tok_acts, tok_grads, pair_ids = (cand_acts, cand_grads, slot_pair)
    query_rows, query_grad_rows = (query_acts, query_grads)
    row_count = tok_acts.shape[0]
    stacked = jnp.concatenate([tok_acts, query_rows], axis=0)
    kept_dev = eigvals.shape[1]
    projected = lax.psum_scatter(
        lax.dot_general(
            basis_in, stacked, (((0,), (1,)), ((), ())), preferred_element_type=jnp.float32
        ),
        "wide",
        scatter_dimension=0,
        tiled=True,
    )
    cand_out = jnp.dot(tok_grads, basis_out, preferred_element_type=jnp.float32)
    query_out = jnp.dot(query_grad_rows, basis_out, preferred_element_type=jnp.float32)
    cand_out, query_out = lax.psum((cand_out, query_out), "wide")
    grad_proj = cand_out.astype(jnp.bfloat16)
    act_proj = projected[:, :row_count]
    query_proj = projected[:, row_count:]
    ratio_table = (
        jnp.einsum(
            "qpi,jqp->iqj",
            query_out.reshape(QUERIES, QPER, KG),
            query_proj.reshape(kept_dev, QUERIES, QPER),
            precision=lax.Precision.HIGHEST,
        )
        / eigvals[:, None, :]
    )
    ratio_table = ratio_table.astype(jnp.bfloat16).reshape(KG, QUERIES * kept_dev)
    block_rows = math.gcd(row_count, 512)
    block_count = row_count // block_rows

    def score_block(block_index):
        product = jnp.dot(grad_proj, ratio_table, preferred_element_type=jnp.float32)
        product = product.reshape(block_rows, QUERIES, kept_dev)
        return jnp.einsum("bqj,jb->bq", product, act_proj, precision=lax.Precision.HIGHEST)

    token_scores = lax.map(score_block, jnp.arange(block_count, dtype=jnp.int32)).reshape(
        row_count, QUERIES
    )
    onehot = (pair_ids[None, :] == jnp.arange(PAIRS, dtype=jnp.int32)[:, None]).astype(jnp.float32)
    partial_value = jnp.dot(onehot, token_scores, precision=lax.Precision.HIGHEST)
    totals = lax.psum_scatter(partial_value, ("wide", "narrow"), scatter_dimension=0, tiled=True)
    score_scale = 1.0 / math.sqrt(
        KG * kept_dev * wide_count * QPER * TOK_DEV * narrow_count / PAIRS
    )
    return totals * score_scale


def solution(mesh):
    in_specs = (
        P(("groups", "narrow"), "wide"),
        P(("groups", "narrow"), "wide"),
        P("groups", "wide"),
        P("groups", "wide"),
        P("wide", None),
        P("wide", None),
        P(None, "wide"),
        P(("groups", "narrow")),
    )
    out_specs = P(("groups", "wide", "narrow"), None)
    return jax.shard_map(
        per_device, mesh=mesh, in_specs=in_specs, out_specs=out_specs, check_vma=False
    )
```

profile of v0, /device:TPU:0, one launch (start us, length us, event | category | flops | bytes accessed | tf_op | source)
XLA Modules:
  0.0 183.8 jit_solution(8438992947743044696)
XLA Ops:
  6.5 0.0 copy-start
  6.5 0.0 copy-start.5
  6.5 0.0 copy-start.1
  6.5 0.0 copy-start.2
  6.5 0.0 copy-start.3
  6.5 0.0 reduce-scatter.2.cloned.1.call-start
  6.6 10.3 %fusion.10 = f32[512,512]{0,1:T(8,128)} fusion(bf16[7168,512]{1,0:T(8,128)(2,1)} %param.12, bf16[256,7168]{1,0:T(8,128)(2,1)} %param.10, bf16[256,7168]{1,0:T(8,128)(2,1)} %param.8), kind=kOutput, calls=%fused_computation.10 | convolution fusion | flops 3772776448 | bytes 15728640 | tf_op jit(solution)/shard_map/dot_general | solution.py:26
  16.9 0.0 reduce-scatter.2.cloned.1.call-update
  16.9 0.0 all-reduce.4.cloned.1.call-start
  17.0 0.0 copy-done
  17.0 0.0 copy-done.1
  17.0 0.4 fusion.20
  17.4 0.8 reshape.17
  18.2 0.0 all-reduce.4.cloned.1.call-update
  18.2 0.0 copy-done.2
  18.2 0.4 fusion.19
  18.7 34.4 %all-reduce.5 = bf16[256,256]{1,0:T(8,128)(2,1)S(1)} all-reduce(f32[256,256]{1,0:T(8,128)S(1)} %fusion.19), channel_id=1, replica_groups=mesh['groups'=2,'wide'=4,'narrow'=4] {'wide'}, use_global_device_ids=true, to_apply=%region_0.0 | all-reduce | flops 65536 | bytes 393216 | tf_op jit(solution)/shard_map/psum | solution.py:35
  53.1 0.0 copy-done.3
  53.1 0.1 copy.10
  53.2 0.0 copy-done.5
  53.2 0.6 dynamic-slice
  54.4 0.0 reduce-scatter.2.cloned.1.call-done
  54.5 1.0 fusion.18
  55.4 35.8 %all-reduce.4.cloned.1.call-done = f32[64,4,256]{2,1,0:T(4,128)} async-done(((f32[64,4,256]{2,1,0:T(4,128)}), f32[64,4,256]{2,1,0:T(4,128)}) %all-reduce.4.cloned.1.call-update) | async-done | bytes 262160 | tf_op jit(solution)/shard_map/psum | solution.py:35
  91.3 7.7 %fusion.21 = f32[64,128,256]{2,1,0:T(8,128)S(1)} fusion(f32[128,64,4]{0,2,1:T(4,128)S(1)} %bitcast.37, f32[64,4,256]{2,1,0:T(4,128)} %all-reduce.4.cloned.1.call-done), kind=kOutput, calls=%fused_computation.21 | convolution fusion | flops 100663296 | bytes 8781824 | tf_op jit(solution)/shard_map/qpi,jqp->iqj/dot_general | solution.py:40
  99.0 1.5 fusion.7
  100.5 0.0 copy-start.4
  100.5 17.5 %fusion.1 = f32[256,1,64]{2,1,0:T(1,128)S(1)} fusion(f32[128,256,1]{0,2,1:T(1,128)S(1)} %bitcast.36, f32[256,64,128]{2,0,1:T(8,128)S(1)} %fusion.7), kind=kOutput, calls=%fused_computation.2 | convolution fusion | flops 25165824 | bytes 8585216 | tf_op jit(solution)/shard_map/while/body/eval_jaxpr/bqj,jb->bq/dot_general | solution.py:55
  118.0 0.0 copy-done.4
  118.0 0.2 fusion.15
  118.2 58.2 %all-reduce = f32[128,64]{1,0:T(8,128)S(1)} all-reduce(f32[128,64]{1,0:T(8,128)S(1)} %fusion.15), channel_id=3, replica_groups=mesh['groups'=2,'wide'=4,'narrow'=4] {'wide','narrow'}, use_global_device_ids=true, to_apply=%region_3.4.clone | all-reduce | flops 8192 | bytes 65536
  176.4 0.6 dynamic-slice_multiply_fusion
Async XLA Ops:
  6.5 10.4 %copy-start = (bf16[2048,256]{1,0:T(8,128)(2,1)S(1)}, bf16[2048,256]{1,0:T(8,128)(2,1)}, u32[]{:S(2)}) copy-start(bf16[2048,256]{1,0:T(8,128)(2,1)} %param.13) | copy-start | bytes 3145732
  6.5 46.6 %copy-start.5 = (u32[32]{0:T(128)S(1)}, u32[32]{0:T(128)}, u32[]{:S(2)}) copy-start(u32[32]{0:T(128)} %constant.12) | copy-start | bytes 388
  6.5 10.4 %copy-start.1 = (bf16[256,2048]{1,0:T(8,128)(2,1)S(1)}, bf16[256,2048]{1,0:T(8,128)(2,1)}, u32[]{:S(2)}) copy-start(bf16[256,2048]{1,0:T(8,128)(2,1)} %param.11) | copy-start | bytes 3145732
  6.5 11.7 %copy-start.2 = (bf16[256,2048]{1,0:T(8,128)(2,1)S(1)}, bf16[256,2048]{1,0:T(8,128)(2,1)}, u32[]{:S(2)}) copy-start(bf16[256,2048]{1,0:T(8,128)(2,1)} %param.9) | copy-start | bytes 3145732
  6.5 46.5 %copy-start.3 = (f32[256,128]{1,0:T(8,128)S(1)}, f32[256,128]{1,0:T(8,128)}, u32[]{:S(2)}) copy-start(f32[256,128]{1,0:T(8,128)} %param.14) | copy-start | bytes 393220
  6.5 47.9 %reduce-scatter.2.cloned.1.call-start = ((), (), s32[]{:S(2)}) async-start(), calls=%async_computation.1 | async-start | bytes 1310720 | tf_op jit(solution)/shard_map/reduce_scatter | solution.py:25
  16.9 74.3 %all-reduce.4.cloned.1.call-start = ((), (), s32[]{:S(2)}) async-start(), calls=%async_computation.2 | async-start | bytes 524288 | tf_op jit(solution)/shard_map/psum | solution.py:35
  100.5 17.5 %copy-start.4 = (s32[256]{0:T(256)S(1)}, s32[256]{0:T(256)}, u32[]{:S(2)}) copy-start(s32[256]{0:T(256)} %param.15) | copy-start | bytes 3076
Sparse Core Ops, SparseCore 0:
  17.0 34.7 reduce-scatter.1
  54.3 36.9 all-reduce.3
where the time goes:
time: 184 us
  blocking collectives  92.5 us (50%)
  matrix products  38.1 us (21%)
  waiting for transfers between devices  35.9 us (20%)
  between operations  14.2 us (8%)
  local copies, waits for them, and re-layouts  2.47 us (1%)
    unnamed x1, blocking collectives  58.2 us
    psum x1, waiting for transfers between devices, per_device(): cand_out, query_out = lax.psum((cand_out, query_out), 'wide')  35.8 us
    psum x1, blocking collectives, per_device(): cand_out, query_out = lax.psum((cand_out, query_out), 'wide')  34.4 us
    dot_general x1, matrix products, score_block(): jnp.einsum('bqj,jb->bq', product, act_proj, precision=lax.Precision.HIGHEST)  17.5 us
    dot_general x1, matrix products, per_device(): lax.dot_general(basis_in, stacked, (((0,), (1,)), ((), ())), preferred_el...  10.3 us
    dot_general x1, matrix products, per_device(): jnp.einsum('qpi,jqp->iqj', query_out.reshape(QUERIES, QPER, KG), query_pr...  7.73 us
  transfers between devices with their start and end apart: 2, of which 1 were waited for; matrix products, arithmetic and copies ran while one was open for 2% of the time, Pallas kernels for 0%

commit v1 on v0

v1 whole, which is shorter than its diff:
```python
import functools
import math

import jax
import jax.numpy as jnp
from jax import lax
from jax.experimental import pallas as pl
from jax.experimental.pallas import tpu as pltpu
from jax.sharding import PartitionSpec as P

QPER = 4
TOK_DEV = 128
PAIRS = 128
MESH = pl.DeviceIdType.MESH
F32 = jnp.float32
BF16 = jnp.bfloat16


def nt_dot(a, b, precision=None):
    return lax.dot_general(
        a, b, (((1,), (1,)), ((), ())), precision=precision, preferred_element_type=F32
    )


def tn_dot(a, b):
    return lax.dot_general(a, b, (((0,), (0,)), ((), ())), preferred_element_type=F32)


def kernel(
    W, N, scale,
    ca, cg, qa, qg, bi, bo, eig, sp,
    out,
    x, vbi, vcg, vqg, vbo, acc,
    g_own, g_send, g_recv, g_all,
    o_send, o_recv, o_all,
    p_send, p_recv, a_send, a_recv,
    qo_all, qp_all,
    qp3, qo3, table, act_t, grad, tsc,
    f_send, f_recv,
    ld_sem, bi_sem, ca_sem, qa_sem,
    gs_s, gs_r, ga_s, ga_r, os_s, os_r, oa_s, oa_r,
    ps_s, ps_r, as_s, as_r, no_s, no_r, np_s, np_r, f_s, f_r,
):
    w = lax.axis_index("wide")
    n = lax.axis_index("narrow")
    me = w * N + n
    C, rows, CK = x.shape
    T = ca.shape[0]
    QN = rows - T
    G = bo.shape[1]
    J = eig.shape[1]
    TW = g_send.shape[1]
    QW = o_send.shape[1]
    PR = f_send.shape[1]
    queries = N * QN // QPER
    wire = g_send.dtype

    q_rows = pl.ds(pl.multiple_of(n * QN, QN), QN)
    loads = [
        pltpu.make_async_copy(bo, vbo, ld_sem.at[0]),
        pltpu.make_async_copy(cg, vcg, ld_sem.at[1]),
        pltpu.make_async_copy(qg.at[q_rows], vqg, ld_sem.at[2]),
    ]
    for c in loads:
        c.start()

    def chunk_copies(c):
        cols = pl.ds(c * CK, CK)
        return (
            pltpu.make_async_copy(bi.at[cols], vbi.at[c], bi_sem.at[c]),
            pltpu.make_async_copy(ca.at[:, cols], x.at[c, pl.ds(0, T)], ca_sem.at[c]),
            pltpu.make_async_copy(qa.at[q_rows, cols], x.at[c, pl.ds(T, QN)], qa_sem.at[c]),
        )

    for c in range(C):
        for copy in chunk_copies(c):
            copy.start()

    barrier = pltpu.get_barrier_semaphore()

    def greet(d, _):
        k = lax.rem(me + d, W * N)
        pl.semaphore_signal(
            barrier, inc=1, device_id={"wide": k // N, "narrow": lax.rem(k, N)},
            device_id_type=MESH,
        )
        return 0

    lax.fori_loop(1, W * N, greet, 0)

    def wide_of(d):
        return lax.rem(w + d, W)

    def scatter(send, recv, s, r, d):
        k = wide_of(d)
        return pltpu.make_async_remote_copy(
            src_ref=send.at[k], dst_ref=recv.at[d], send_sem=s.at[d], recv_sem=r.at[d],
            device_id={"wide": k}, device_id_type=MESH,
        )

    def gather(buf, s, r, d):
        return pltpu.make_async_remote_copy(
            src_ref=buf.at[w], dst_ref=buf.at[w], send_sem=s.at[d], recv_sem=r.at[d],
            device_id={"wide": wide_of(d)}, device_id_type=MESH,
        )

    def share(buf, s, r, d):
        return pltpu.make_async_remote_copy(
            src_ref=buf.at[n], dst_ref=buf.at[n], send_sem=s.at[d], recv_sem=r.at[d],
            device_id={"narrow": lax.rem(n + d, N)}, device_id_type=MESH,
        )

    def final(d):
        k = lax.rem(me + d, W * N)
        return pltpu.make_async_remote_copy(
            src_ref=f_send.at[k], dst_ref=f_recv.at[d], send_sem=f_s.at[d], recv_sem=f_r.at[d],
            device_id={"wide": k // N, "narrow": lax.rem(k, N)}, device_id_type=MESH,
        )

    def each(count, make, what):
        def body(d, _):
            getattr(make(d), what)()
            return 0

        lax.fori_loop(1, count, body, 0)

    grad_rs = functools.partial(scatter, g_send, g_recv, gs_s, gs_r)
    out_rs = functools.partial(scatter, o_send, o_recv, os_s, os_r)
    proj_rs = functools.partial(scatter, p_send, p_recv, ps_s, ps_r)
    act_rs = functools.partial(scatter, a_send, a_recv, as_s, as_r)
    grad_ag = functools.partial(gather, g_all, ga_s, ga_r)
    out_ag = functools.partial(gather, o_all, oa_s, oa_r)
    out_sh = functools.partial(share, qo_all, no_s, no_r)
    proj_sh = functools.partial(share, qp_all, np_s, np_r)

    for c in loads:
        c.wait()
    part = jnp.dot(vcg[...], vbo[...], preferred_element_type=F32)
    for k in range(W):
        block = part[k * TW : (k + 1) * TW]
        g_own[k] = block
        g_send[k] = block.astype(wire)
    part = jnp.dot(vqg[...], vbo[...], preferred_element_type=F32)
    for k in range(W):
        o_send[k] = part[k * QW : (k + 1) * QW]

    pl.semaphore_wait(barrier, W * N - 1)
    each(W, out_rs, "start")
    each(W, grad_rs, "start")

    def project(c, _):
        cols = pl.ds(c * CK, CK)
        pltpu.make_async_copy(bi.at[cols], vbi.at[c], bi_sem.at[c]).wait()
        pltpu.make_async_copy(ca.at[:, cols], x.at[c, pl.ds(0, T)], ca_sem.at[c]).wait()
        pltpu.make_async_copy(
            qa.at[q_rows, cols], x.at[c, pl.ds(T, QN)], qa_sem.at[c]
        ).wait()
        acc[...] += jnp.dot(x[c], vbi[c], preferred_element_type=F32)
        return 0

    acc[...] = jnp.zeros_like(acc)
    mid = max(C - 2, 0)
    lax.fori_loop(0, mid, project, 0)

    each(W, out_rs, "wait_recv")
    total = o_send[w]
    for d in range(1, W):
        total = total + o_recv[d]
    o_all[w] = total
    each(W, out_ag, "start")
    each(W, grad_rs, "wait_recv")
    total = g_own[w]
    for d in range(1, W):
        total = total + g_recv[d].astype(F32)
    g_all[w] = total.astype(BF16).astype(wire)
    each(W, grad_ag, "start")

    lax.fori_loop(mid, C, project, 0)

    for k in range(W):
        p_send[k] = acc[T:, k * J : (k + 1) * J]
    each(W, proj_rs, "start")
    for k in range(W):
        a_send[k] = acc[:T, k * J : (k + 1) * J].astype(BF16)
    each(W, act_rs, "start")

    recip = (1.0 / eig[...]).T
    each(W, out_ag, "wait_recv")
    for k in range(W):
        qo_all[n, k * QW : (k + 1) * QW, :] = o_all[k]
    each(N, out_sh, "start")
    each(W, proj_rs, "wait_recv")
    total = p_send[w]
    for d in range(1, W):
        total = total + p_recv[d]
    qp_all[n] = total
    each(N, proj_sh, "start")

    each(N, out_sh, "wait_recv")
    groups, three, _ = qp3.shape
    GT = three // 3
    per = QN // GT
    for g in range(groups):
        at, lo = g // per, (g % per) * GT
        val = qo_all[at, lo : lo + GT, :]
        hi = val.astype(BF16)
        low = (val - hi.astype(F32)).astype(BF16)
        qo3[g, 0:GT] = hi
        qo3[g, GT : 2 * GT] = low
        qo3[g, 2 * GT :] = hi
    each(N, proj_sh, "wait_recv")
    for g in range(groups):
        at, lo = g // per, (g % per) * GT
        val = qp_all[at, lo : lo + GT, :]
        hi = val.astype(BF16)
        low = (val - hi.astype(F32)).astype(BF16)
        qp3[g, 0:GT] = hi
        qp3[g, GT : 2 * GT] = hi
        qp3[g, 2 * GT :] = low

    GQ = GT // QPER
    token = lax.rem(lax.broadcasted_iota(jnp.int32, (three, G), 0), GT)

    def build(g, _):
        left = qp3[g]
        right = qo3[g].astype(F32)
        for k in range(GQ):
            mine = jnp.where((token >= k * QPER) & (token < (k + 1) * QPER), right, 0.0)
            block = tn_dot(left, mine.astype(BF16)) * recip
            table[g, k * J : (k + 1) * J, :] = block.astype(BF16)
        return 0

    lax.fori_loop(0, groups, build, 0)

    each(W, grad_ag, "wait_recv")
    for k in range(W):
        grad[k * TW : (k + 1) * TW, :] = g_all[k].astype(F32)
    grads = grad[...].astype(BF16)
    tsc[...] = jnp.zeros_like(tsc)
    each(W, act_rs, "wait_recv")
    own = a_send[w].astype(F32)
    for d in range(1, W):
        own = own + a_recv[d].astype(F32)
    act_t[...] = own.T

    def score(g, _):
        h = nt_dot(table[g], grads)
        for k in range(GQ):
            rowsum = jnp.sum(h[k * J : (k + 1) * J] * act_t[...], axis=0, keepdims=True)
            tsc[pl.ds(g * GQ + k, 1), :] = rowsum
        return 0

    lax.fori_loop(0, groups, score, 0)

    pair = lax.broadcasted_iota(jnp.int32, (PAIRS, T), 0)
    onehot = (pair == sp[...]).astype(F32)
    value = nt_dot(onehot, tsc[...], lax.Precision.HIGHEST)
    for k in range(W * N):
        f_send[k] = value[k * PR : (k + 1) * PR]
    each(W * N, final, "start")
    each(W * N, final, "wait_recv")
    total = f_send[me]
    for d in range(1, W * N):
        total = total + f_recv[d]
    out[...] = total[:, :queries] * scale

    for count, make in (
        (W, out_rs), (W, grad_rs), (W, out_ag), (W, grad_ag), (W, proj_rs), (W, act_rs),
        (N, out_sh), (N, proj_sh), (W * N, final),
    ):
        each(count, make, "wait_send")


def per_device(
    cand_acts, cand_grads, query_acts, query_grads, basis_in, basis_out, eigvals, slot_pair
):
    W = lax.axis_size("wide")
    N = lax.axis_size("narrow")
    T, F = cand_acts.shape
    D = cand_grads.shape[1]
    Q = query_acts.shape[0]
    KA = basis_in.shape[1]
    G, J = eigvals.shape
    QN = Q // N
    TW, QW = T // W, QN // W
    PR = PAIRS // (W * N)
    queries = Q // QPER
    qpad = -(-queries // 128) * 128
    C = next(c for c in range(max(F // 1024, 1), F + 1) if F % (c * 128) == 0)
    CK = F // C
    GT = 32
    groups = Q // GT
    wire = BF16 if TW % 16 == 0 else F32
    scale = 1.0 / math.sqrt(G * J * W * QPER * TOK_DEV * N / PAIRS)
    vm = pltpu.VMEM
    dma = pltpu.SemaphoreType.DMA
    scratch = [
        vm((C, T + QN, CK), BF16), vm((C, CK, KA), BF16), vm((T, D), BF16), vm((QN, D), BF16),
        vm((D, G), BF16), vm((T + QN, KA), F32),
        vm((W, TW, G), F32), vm((W, TW, G), wire), vm((W, TW, G), wire), vm((W, TW, G), wire),
        vm((W, QW, G), F32), vm((W, QW, G), F32), vm((W, QW, G), F32),
        vm((W, QN, J), F32), vm((W, QN, J), F32), vm((W, T, J), BF16), vm((W, T, J), BF16),
        vm((N, QN, G), F32), vm((N, QN, J), F32),
        vm((groups, 3 * GT, J), BF16), vm((groups, 3 * GT, G), BF16),
        vm((groups, GT // QPER * J, G), BF16), vm((J, T), F32), vm((T, G), F32), vm((qpad, T), F32),
        vm((W * N, PR, qpad), F32), vm((W * N, PR, qpad), F32),
        dma((3,)), dma((C,)), dma((C,)), dma((C,)),
    ] + [dma((W,))] * 12 + [dma((N,))] * 4 + [dma((W * N,))] * 2
    hbm = pl.BlockSpec(memory_space=pl.ANY)
    vmem = pl.BlockSpec(memory_space=pltpu.VMEM)
    return pl.pallas_call(
        functools.partial(kernel, W, N, scale),
        out_shape=jax.ShapeDtypeStruct((PR, queries), F32),
        in_specs=[hbm] * 6 + [vmem] * 2,
        out_specs=vmem,
        scratch_shapes=scratch,
        compiler_params=pltpu.CompilerParams(
            collective_id=0, has_side_effects=True, vmem_limit_bytes=50 * 2**20
        ),
        cost_estimate=pl.CostEstimate(
            flops=2 * (T + QN) * F * KA, bytes_accessed=2 * F * (KA + T + QN), transcendentals=0
        ),
    )(
        cand_acts, cand_grads, query_acts, query_grads, basis_in, basis_out, eigvals,
        slot_pair.reshape(1, T),
    )


def solution(mesh):
    in_specs = (
        P(("groups", "narrow"), "wide"),
        P(("groups", "narrow"), "wide"),
        P("groups", "wide"),
        P("groups", "wide"),
        P("wide", None),
        P("wide", None),
        P(None, "wide"),
        P(("groups", "narrow")),
    )
    out_specs = P(("groups", "wide", "narrow"), None)
    return jax.shard_map(
        per_device, mesh=mesh, in_specs=in_specs, out_specs=out_specs, check_vma=False
    )
```

time: 184 us -> 43.1 us (0.23)
  blocking collectives: 92.5 us -> 0 us
  matrix products: 38.1 us -> 0 us
  Pallas kernels: 0 us -> 37 us
  waiting for transfers between devices: 35.9 us -> 0 us
  between operations: 14.2 us -> 0.01 us
  local copies, waits for them, and re-layouts: 2.47 us -> 5.85 us
    unnamed x1 -> x0, blocking collectives: 58.2 us -> none
    dot_general x7 -> x0, matrix products: 38.1 us -> none  [the longest x1 17.5 us: score_block(): jnp.einsum('bqj,jb->bq', product, act_proj, precision=lax.Precision.HIGHEST)]
    pallas_call x0 -> x1, Pallas kernels: none -> 37 us  [per_device(): pl.pallas_call(functools.partial(kernel, W, N, scale), out_shape=jax.Shap...]
    psum x1 -> x0, waiting for transfers between devices: 35.8 us -> none  [per_device(): cand_out, query_out = lax.psum((cand_out, query_out), 'wide')]
    psum x1 -> x0, blocking collectives: 34.4 us -> none  [per_device(): cand_out, query_out = lax.psum((cand_out, query_out), 'wide')]
    unnamed x14 -> x11, local copies, waits for them, and re-layouts: 0.7 us -> 5.85 us
  transfers between devices with their start and end apart: 2 -> 0, of which waited for: 1 -> 0; matrix products, arithmetic and copies ran while one was open for 2% -> 0% of each run, Pallas kernels for 0% -> 0%
where the time goes in v1:
time: 43.1 us; the launch traced here: 42.9 us
  Pallas kernels  37 us (86%)
  local copies, waits for them, and re-layouts  5.85 us (14%)
    pallas_call x1, Pallas kernels, per_device(): pl.pallas_call(functools.partial(kernel, W, N, scale), out_shape=jax.Shap...  37 us
    unnamed x11, local copies, waits for them, and re-layouts  5.85 us

profile of v1, /device:TPU:0, one launch (start us, length us, event | category | flops | bytes accessed | tf_op | source)
XLA Modules:
  0.0 42.9 jit_solution(4480441979160733201)
XLA Ops:
  0.0 0.0 copy-start
  0.0 1.2 %copy-done = bf16[256,2048]{1,0:T(8,128)(2,1)S(1)} copy-done((bf16[256,2048]{1,0:T(8,128)(2,1)S(1)}, bf16[256,2048]{1,0:T(8,128)(2,1)}, u32[]{:S(2)}) %copy-start) | copy-done | bytes 1048600
  1.2 0.0 copy-start.1
  1.2 1.2 %copy-done.1 = bf16[256,2048]{1,0:T(8,128)(2,1)S(1)} copy-done((bf16[256,2048]{1,0:T(8,128)(2,1)S(1)}, bf16[256,2048]{1,0:T(8,128)(2,1)}, u32[]{:S(2)}) %copy-start.1) | copy-done | bytes 1048600
  2.5 0.0 copy-start.2
  2.5 1.2 %copy-done.2 = bf16[2048,256]{1,0:T(8,128)(2,1)S(1)} copy-done((bf16[2048,256]{1,0:T(8,128)(2,1)S(1)}, bf16[2048,256]{1,0:T(8,128)(2,1)}, u32[]{:S(2)}) %copy-start.2) | copy-done | bytes 1048600
  3.7 0.0 copy-start.3
  3.7 0.9 %copy-done.3 = f32[256,128]{1,0:T(8,128)S(1)} copy-done((f32[256,128]{1,0:T(8,128)S(1)}, f32[256,128]{1,0:T(8,128)}, u32[]{:S(2)}) %copy-start.3) | copy-done | bytes 131096
  4.6 0.0 copy-start.4
  4.6 0.7 %copy-done.4 = s32[256]{0:T(256)S(1)} copy-done((s32[256]{0:T(256)S(1)}, s32[256]{0:T(256)}, u32[]{:S(2)}) %copy-start.4) | copy-done | bytes 1048
  5.3 37.0 %shard_map.82 = f32[8,64]{1,0:T(8,128)S(1)} custom-call(bf16[256,7168]{1,0:T(8,128)(2,1)} %ca.1, bf16[256,2048]{1,0:T(8,128)(2,1)S(1)} %copy-done, bf16[256,7168]{1,0:T(8,128)(2,1)} %qa.1, bf16[256,2048]{1,0:T(8,128)(2,1)S(1)} %copy-done.1, bf16[7168,512]{1,0:T(8,128)(2,1)} %bi.1, bf16[2048,256]{1,0:T(8,128)(2,1)S(1)} %copy-done.2, ...), custom_call_target="tpu_custom_call" | custom-call | flops 2348810240 | bytes 11927552 | tf_op jit(solution)/shard_map/pallas_call | solution.py:311
  42.3 0.6 %copy.10 = f32[8,64]{1,0:T(8,128)} copy(f32[8,64]{1,0:T(8,128)S(1)} %shard_map.82) | data formatting | bytes 4096
Async XLA Ops:
  0.0 1.2 %copy-start = (bf16[256,2048]{1,0:T(8,128)(2,1)S(1)}, bf16[256,2048]{1,0:T(8,128)(2,1)}, u32[]{:S(2)}) copy-start(bf16[256,2048]{1,0:T(8,128)(2,1)} %cg.1) | copy-start | bytes 3145732
  1.2 1.2 %copy-start.1 = (bf16[256,2048]{1,0:T(8,128)(2,1)S(1)}, bf16[256,2048]{1,0:T(8,128)(2,1)}, u32[]{:S(2)}) copy-start(bf16[256,2048]{1,0:T(8,128)(2,1)} %qg.1) | copy-start | bytes 3145732
  2.5 1.2 %copy-start.2 = (bf16[2048,256]{1,0:T(8,128)(2,1)S(1)}, bf16[2048,256]{1,0:T(8,128)(2,1)}, u32[]{:S(2)}) copy-start(bf16[2048,256]{1,0:T(8,128)(2,1)} %bo.1) | copy-start | bytes 3145732
  3.7 0.9 %copy-start.3 = (f32[256,128]{1,0:T(8,128)S(1)}, f32[256,128]{1,0:T(8,128)}, u32[]{:S(2)}) copy-start(f32[256,128]{1,0:T(8,128)} %eig.1) | copy-start | bytes 393220
  4.6 0.7 %copy-start.4 = (s32[256]{0:T(256)S(1)}, s32[256]{0:T(256)}, u32[]{:S(2)}) copy-start(s32[256]{0:T(256)} %param.15) | copy-start | bytes 3076

commit v2 on v1

--- a/solution.py
+++ b/solution.py
@@ -28,14 +28,14 @@
 
 def kernel(
     W, N, scale,
-    ca, cg, qa, qg, bi, bo, eig, sp,
+    ca, cg, qa, qg, bi, bo, eig_hbm, sp_hbm,
     out,
-    x, vbi, vcg, vqg, vbo, acc,
+    eig, sp, x, vbi, vcg, vqg, vbo, acc,
     g_own, g_send, g_recv, g_all,
     o_send, o_recv, o_all,
     p_send, p_recv, a_send, a_recv,
     qo_all, qp_all,
-    qp3, qo3, table, act_t, grad, tsc,
+    table, act_t, grad, tsc,
     f_send, f_recv,
     ld_sem, bi_sem, ca_sem, qa_sem,
     gs_s, gs_r, ga_s, ga_r, os_s, os_r, oa_s, oa_r,
@@ -58,8 +58,12 @@
     q_rows = pl.ds(pl.multiple_of(n * QN, QN), QN)
     loads = [
         pltpu.make_async_copy(bo, vbo, ld_sem.at[0]),
-        pltpu.make_async_copy(cg, vcg, ld_sem.at[1]),
-        pltpu.make_async_copy(qg.at[q_rows], vqg, ld_sem.at[2]),
+        pltpu.make_async_copy(qg.at[q_rows], vqg, ld_sem.at[1]),
+        pltpu.make_async_copy(cg, vcg, ld_sem.at[2]),
+    ]
+    late = [
+        pltpu.make_async_copy(eig_hbm, eig, ld_sem.at[3]),
+        pltpu.make_async_copy(sp_hbm, sp, ld_sem.at[4]),
     ]
     for c in loads:
         c.start()
@@ -75,6 +79,8 @@
     for c in range(C):
         for copy in chunk_copies(c):
             copy.start()
+    for c in late:
+        c.start()
 
     barrier = pltpu.get_barrier_semaphore()
 
@@ -133,20 +139,17 @@
     out_sh = functools.partial(share, qo_all, no_s, no_r)
     proj_sh = functools.partial(share, qp_all, np_s, np_r)
 
-    for c in loads:
-        c.wait()
+    loads[0].wait()
+    loads[1].wait()
+    part = jnp.dot(vqg[...], vbo[...], preferred_element_type=F32)
+    for k in range(W):
+        o_send[k] = part[k * QW : (k + 1) * QW]
+    loads[2].wait()
     part = jnp.dot(vcg[...], vbo[...], preferred_element_type=F32)
     for k in range(W):
         block = part[k * TW : (k + 1) * TW]
         g_own[k] = block
         g_send[k] = block.astype(wire)
-    part = jnp.dot(vqg[...], vbo[...], preferred_element_type=F32)
-    for k in range(W):
-        o_send[k] = part[k * QW : (k + 1) * QW]
-
-    pl.semaphore_wait(barrier, W * N - 1)
-    each(W, out_rs, "start")
-    each(W, grad_rs, "start")
 
     def project(c, _):
         cols = pl.ds(c * CK, CK)
@@ -159,8 +162,12 @@
         return 0
 
     acc[...] = jnp.zeros_like(acc)
-    mid = max(C - 2, 0)
-    lax.fori_loop(0, mid, project, 0)
+    first, mid = C * 2 // 7, C * 5 // 7
+    lax.fori_loop(0, first, project, 0)
+    pl.semaphore_wait(barrier, W * N - 1)
+    each(W, out_rs, "start")
+    each(W, grad_rs, "start")
+    lax.fori_loop(first, mid, project, 0)
 
     each(W, out_rs, "wait_recv")
     total = o_send[w]
@@ -168,27 +175,30 @@
         total = total + o_recv[d]
     o_all[w] = total
     each(W, out_ag, "start")
+    lax.fori_loop(mid, C, project, 0)
+
+    for k in range(W):
+        p_send[k] = acc[T:, k * J : (k + 1) * J]
+    each(W, proj_rs, "start")
+
+    each(W, out_ag, "wait_recv")
+    for k in range(W):
+        qo_all[n, k * QW : (k + 1) * QW, :] = o_all[k]
+    each(N, out_sh, "start")
+
     each(W, grad_rs, "wait_recv")
     total = g_own[w]
     for d in range(1, W):
         total = total + g_recv[d].astype(F32)
     g_all[w] = total.astype(BF16).astype(wire)
     each(W, grad_ag, "start")
-
-    lax.fori_loop(mid, C, project, 0)
-
-    for k in range(W):
-        p_send[k] = acc[T:, k * J : (k + 1) * J]
-    each(W, proj_rs, "start")
     for k in range(W):
         a_send[k] = acc[:T, k * J : (k + 1) * J].astype(BF16)
     each(W, act_rs, "start")
 
+    for c in late:
+        c.wait()
     recip = (1.0 / eig[...]).T
-    each(W, out_ag, "wait_recv")
-    for k in range(W):
-        qo_all[n, k * QW : (k + 1) * QW, :] = o_all[k]
-    each(N, out_sh, "start")
     each(W, proj_rs, "wait_recv")
     total = p_send[w]
     for d in range(1, W):
@@ -196,34 +206,29 @@
     qp_all[n] = total
     each(N, proj_sh, "start")
 
-    each(N, out_sh, "wait_recv")
-    groups, three, _ = qp3.shape
-    GT = three // 3
+    groups, GT = table.shape[0], table.shape[1] // J * QPER
+    three = 3 * GT
     per = QN // GT
-    for g in range(groups):
-        at, lo = g // per, (g % per) * GT
-        val = qo_all[at, lo : lo + GT, :]
-        hi = val.astype(BF16)
-        low = (val - hi.astype(F32)).astype(BF16)
-        qo3[g, 0:GT] = hi
-        qo3[g, GT : 2 * GT] = low
-        qo3[g, 2 * GT :] = hi
-    each(N, proj_sh, "wait_recv")
-    for g in range(groups):
-        at, lo = g // per, (g % per) * GT
-        val = qp_all[at, lo : lo + GT, :]
-        hi = val.astype(BF16)
-        low = (val - hi.astype(F32)).astype(BF16)
-        qp3[g, 0:GT] = hi
-        qp3[g, GT : 2 * GT] = hi
-        qp3[g, 2 * GT :] = low
-
     GQ = GT // QPER
     token = lax.rem(lax.broadcasted_iota(jnp.int32, (three, G), 0), GT)
 
-    def build(g, _):
-        left = qp3[g]
-        right = qo3[g].astype(F32)
+    def build(step, _):
+        d = step // per
+
+        @pl.when((d > 0) & (lax.rem(step, per) == 0))
+        def _():
+            out_sh(d).wait_recv()
+            proj_sh(d).wait_recv()
+
+        at = lax.rem(n + N - d, N)
+        lo = pl.multiple_of(lax.rem(step, per) * GT, GT)
+        val = qp_all[at, pl.ds(lo, GT), :]
+        hi = val.astype(BF16).astype(F32)
+        left = jnp.concatenate([hi, hi, val - hi], axis=0).astype(BF16)
+        val = qo_all[at, pl.ds(lo, GT), :]
+        hi = val.astype(BF16).astype(F32)
+        right = jnp.concatenate([hi, val - hi, hi], axis=0)
+        g = at * per + lax.rem(step, per)
         for k in range(GQ):
             mine = jnp.where((token >= k * QPER) & (token < (k + 1) * QPER), right, 0.0)
             block = tn_dot(left, mine.astype(BF16)) * recip
@@ -295,27 +300,27 @@
     vm = pltpu.VMEM
     dma = pltpu.SemaphoreType.DMA
     scratch = [
+        vm((G, J), F32), vm((1, T), jnp.int32),
         vm((C, T + QN, CK), BF16), vm((C, CK, KA), BF16), vm((T, D), BF16), vm((QN, D), BF16),
         vm((D, G), BF16), vm((T + QN, KA), F32),
         vm((W, TW, G), F32), vm((W, TW, G), wire), vm((W, TW, G), wire), vm((W, TW, G), wire),
         vm((W, QW, G), F32), vm((W, QW, G), F32), vm((W, QW, G), F32),
         vm((W, QN, J), F32), vm((W, QN, J), F32), vm((W, T, J), BF16), vm((W, T, J), BF16),
         vm((N, QN, G), F32), vm((N, QN, J), F32),
-        vm((groups, 3 * GT, J), BF16), vm((groups, 3 * GT, G), BF16),
         vm((groups, GT // QPER * J, G), BF16), vm((J, T), F32), vm((T, G), F32), vm((qpad, T), F32),
         vm((W * N, PR, qpad), F32), vm((W * N, PR, qpad), F32),
-        dma((3,)), dma((C,)), dma((C,)), dma((C,)),
+        dma((5,)), dma((C,)), dma((C,)), dma((C,)),
     ] + [dma((W,))] * 12 + [dma((N,))] * 4 + [dma((W * N,))] * 2
     hbm = pl.BlockSpec(memory_space=pl.ANY)
     vmem = pl.BlockSpec(memory_space=pltpu.VMEM)
     return pl.pallas_call(
         functools.partial(kernel, W, N, scale),
         out_shape=jax.ShapeDtypeStruct((PR, queries), F32),
-        in_specs=[hbm] * 6 + [vmem] * 2,
+        in_specs=[hbm] * 8,
         out_specs=vmem,
         scratch_shapes=scratch,
         compiler_params=pltpu.CompilerParams(
-            collective_id=0, has_side_effects=True, vmem_limit_bytes=50 * 2**20
+            collective_id=0, has_side_effects=True, vmem_limit_bytes=63 * 2**20
         ),
         cost_estimate=pl.CostEstimate(
             flops=2 * (T + QN) * F * KA, bytes_accessed=2 * F * (KA + T + QN), transcendentals=0

time: 43.1 us -> 37.8 us (0.88)
  local copies, waits for them, and re-layouts: 5.85 us -> 1.28 us
  Pallas kernels: 37 us -> 36.3 us
    unnamed x11 -> x1, local copies, waits for them, and re-layouts: 5.85 us -> 1.28 us
    pallas_call x1, Pallas kernels: 37 us -> 36.3 us  [per_device(): pl.pallas_call(functools.partial(kernel, W, N, scale), out_shape=jax.Shap...]
where the time goes in v2:
time: 37.8 us; the launch traced here: 37.6 us
  Pallas kernels  36.3 us (96%)
  local copies, waits for them, and re-layouts  1.28 us (3%)
    pallas_call x1, Pallas kernels, per_device(): pl.pallas_call(functools.partial(kernel, W, N, scale), out_shape=jax.Shap...  36.3 us
    unnamed x1, local copies, waits for them, and re-layouts  1.28 us

profile of v2, /device:TPU:0, one launch (start us, length us, event | category | flops | bytes accessed | tf_op | source)
XLA Modules:
  0.0 37.6 jit_solution(14651089856341394679)
XLA Ops:
  0.0 36.3 %shard_map.82 = f32[8,64]{1,0:T(8,128)} custom-call(bf16[256,7168]{1,0:T(8,128)(2,1)} %ca.1, bf16[256,2048]{1,0:T(8,128)(2,1)} %cg.1, bf16[256,7168]{1,0:T(8,128)(2,1)} %qa.1, bf16[256,2048]{1,0:T(8,128)(2,1)} %qg.1, bf16[7168,512]{1,0:T(8,128)(2,1)} %bi.1, bf16[2048,256]{1,0:T(8,128)(2,1)} %bo.1, f32[256,128]{1,0:T(8,128)} %eig_hbm.1, s32[1,256]{1,0:T(1,128)} %bitcast.1), custom_call_target="tpu_custom_call" | custom-call | flops 2348810240 | bytes 11927552 | tf_op jit(solution)/shard_map/pallas_call | solution.py:316
  36.3 1.3 %copy.10 = f32[8,64]{1,0:T(8,128)} copy(f32[8,64]{1,0:T(8,128)} %shard_map.82) | data formatting | bytes 4096

commit v3 on v2

--- a/solution.py
+++ b/solution.py
@@ -162,7 +162,7 @@
         return 0
 
     acc[...] = jnp.zeros_like(acc)
-    first, mid = C * 2 // 7, C * 5 // 7
+    first, mid = 0, C * 6 // 7
     lax.fori_loop(0, first, project, 0)
     pl.semaphore_wait(barrier, W * N - 1)
     each(W, out_rs, "start")

time: 37.8 us -> 36.6 us (0.968)
  Pallas kernels: 36.3 us -> 35.1 us
    pallas_call x1, Pallas kernels: 36.3 us -> 35.1 us  [per_device(): pl.pallas_call(functools.partial(kernel, W, N, scale), out_shape=jax.Shap...]
where the time goes in v3:
time: 36.6 us; the launch traced here: 36.4 us
  Pallas kernels  35.1 us (96%)
  local copies, waits for them, and re-layouts  1.28 us (3%)
    pallas_call x1, Pallas kernels, per_device(): pl.pallas_call(functools.partial(kernel, W, N, scale), out_shape=jax.Shap...  35.1 us
    unnamed x1, local copies, waits for them, and re-layouts  1.28 us

profile of v3, /device:TPU:0, one launch (start us, length us, event | category | flops | bytes accessed | tf_op | source)
XLA Modules:
  0.0 36.4 jit_solution(3210267587846018765)
XLA Ops:
  0.0 35.1 %shard_map.82 = f32[8,64]{1,0:T(8,128)} custom-call(bf16[256,7168]{1,0:T(8,128)(2,1)} %ca.1, bf16[256,2048]{1,0:T(8,128)(2,1)} %cg.1, bf16[256,7168]{1,0:T(8,128)(2,1)} %qa.1, bf16[256,2048]{1,0:T(8,128)(2,1)} %qg.1, bf16[7168,512]{1,0:T(8,128)(2,1)} %bi.1, bf16[2048,256]{1,0:T(8,128)(2,1)} %bo.1, f32[256,128]{1,0:T(8,128)} %eig_hbm.1, s32[1,256]{1,0:T(1,128)} %bitcast.1), custom_call_target="tpu_custom_call" | custom-call | flops 2348810240 | bytes 11927552 | tf_op jit(solution)/shard_map/pallas_call | solution.py:316
  35.1 1.3 %copy.10 = f32[8,64]{1,0:T(8,128)} copy(f32[8,64]{1,0:T(8,128)} %shard_map.82) | data formatting | bytes 4096
